TPU v7x, 256 devices: a whole 4x4x8 slice. The times are simulated.
256 devices in a mesh: ctx: 128 (over y, x_lo, z, core), head: 2 (over x_hi).
Axes of the slice: x: 4 (x_hi: 2, x_lo: 2; x = x_hi * 2 + x_lo), y: 4, z: 8, core: 2. Of those that a mesh axis runs over, the one named last changes fastest.
Arguments:
- q_raw: bfloat16 [32768, 4096], P('ctx', 'head'), may hold values from -8 to 8
- k_raw: bfloat16 [32768, 4096], P('ctx', 'head'), may hold values from -8 to 8
- v_raw: bfloat16 [32768, 4096], P('ctx', 'head'), may hold values from -8 to 8
- g_raw: bfloat16 [32768, 4096], P('ctx', 'head'), may hold values from -6 to 6
- short_filters: float32 [4, 3, 4096], P(None, None, 'head'), may hold values from 0.2 to 1
- long_filter: float32 [7, 4096], P(None, 'head'), may hold values from -2 to 2
- out_gain: float32 [4096], P('head'), may hold values from 0.25 to 1.75
- block_lists: int32 [256, 7], replicated, may hold values from -1 to 255, as said below
Outputs:
- normed: bfloat16 [32768, 4096], P('ctx', 'head')
Inputs may be any that keep to these rules, and one draw needn't show every extreme that they name: `block_lists`: row i holds in slot t < 3 the block i - t, or -1 where i - t < 0. In slot 3 + s it holds either -1 or p + s * 64, the latter only where that is at most i - 3, with one offset p of 0 to 60 for the whole array. Each row keeps or drops each such global entry by its own drawn choice. The last row keeps all of them.
All inputs are finite; a program needn't handle non-finite values.
Results may differ from a plain program's by a relative error of at most 0.0086.
Values may be sent and summed in bfloat16 or wider, within the bound.
A program may use at most 128 MiB of HBM per device.

v0:
```python
import math

import jax
import jax.numpy as jnp
from jax import lax
from jax.sharding import PartitionSpec as P

D = 4096
HS = 128
BLK = 128
BAND = 3
NGLOB = 4
TAPS = 3
TAPS_LONG = 7


def from_behind(block, axis, distance):
    devices = range(lax.axis_size(axis))
    route = [(i - distance, i) for i in devices if i - distance in devices]
    return lax.ppermute(block, axis, route)


def broadcast(value, axis, source):
    kept = jnp.where(lax.axis_index(axis) == source, value, 0).astype(value.dtype)
    return lax.psum(kept, axis)


def causal_filter(extended, weights, count_rows):
    tap_count = weights.shape[0]
    result = jnp.zeros((count_rows, extended.shape[1]), jnp.float32)
    for offset in range(tap_count):
        begin_row = tap_count - 1 - offset
        result = result + weights[offset] * extended[begin_row : begin_row + count_rows].astype(
            jnp.float32
        )
    return result


def per_device(q_raw, k_raw, v_raw, g_raw, short_filters, long_filter, out_gain, block_lists):
    row_count, width_here = q_raw.shape
    heads_here = width_here // HS
    blocks_here = row_count // BLK
    streams = (q_raw, k_raw, v_raw, g_raw)
    before = from_behind(
        (
            q_raw[row_count - TAPS + 1 :],
            k_raw[row_count - TAPS + 1 :],
            v_raw[row_count - TAPS + 1 :],
            g_raw[row_count - TAPS + 1 :],
        ),
        "ctx",
        1,
    )
    features = [
        causal_filter(
            jnp.concatenate([before[stream_index], streams[stream_index]], 0),
            short_filters[stream_index],
            row_count,
        )
        for stream_index in range(4)
    ]
    gated_inner = features[3] * features[2]
    inner_before = from_behind(gated_inner[row_count - TAPS_LONG + 1 :], "ctx", 1)
    value_feat = causal_filter(
        jnp.concatenate([inner_before, gated_inner], 0), long_filter, row_count
    ).astype(jnp.bfloat16)
    query_feat = features[0].astype(jnp.bfloat16)
    key_feat = features[1].astype(jnp.bfloat16)
    whole_key, whole_value = from_behind((key_feat, value_feat), "ctx", 1)
    ext_key = jnp.concatenate([whole_key, key_feat], 0)
    ext_value = jnp.concatenate([whole_value, value_feat], 0)
    first_block = lax.axis_index("ctx") * blocks_here
    block_ids = first_block + jnp.arange(blocks_here, dtype=jnp.int32)
    query_blocks = query_feat.reshape(blocks_here, BLK, heads_here, HS)
    causal_mask = jnp.arange(BLK)[:, None] >= jnp.arange(BLK)[None, :]
    row_top = jnp.full((blocks_here, heads_here, BLK), -jnp.inf, jnp.float32)
    band_scores = []
    band_values = []
    for band_step in range(BAND):
        key_window = ext_key[band_step * BLK : band_step * BLK + row_count].reshape(
            blocks_here, BLK, heads_here, HS
        )
        scores = jnp.einsum(
            "bqhd,bkhd->bhqk", query_blocks, key_window, preferred_element_type=jnp.float32
        ) / math.sqrt(HS)
        allowed = (block_ids - (BAND - 1) + band_step >= 0)[:, None, None, None]
        if band_step == BAND - 1:
            allowed = allowed & causal_mask[None, None, :, :]
        scores = jnp.where(allowed, scores, -jnp.inf)
        row_top = jnp.maximum(row_top, jnp.max(scores, axis=3))
        band_scores.append(scores)
        band_values.append(
            ext_value[band_step * BLK : band_step * BLK + row_count].reshape(
                blocks_here, BLK, heads_here, HS
            )
        )
    list_rows = block_lists.shape[0]
    stride_blocks = list_rows // NGLOB
    phase = block_lists[list_rows - 1, BAND]
    global_key_list = []
    global_value_list = []
    for slot_index in range(NGLOB):
        global_index = phase + slot_index * stride_blocks
        owner = global_index // blocks_here
        begin_row = global_index % blocks_here * BLK
        got_key, got_value = (
            broadcast(lax.dynamic_slice_in_dim(key_feat, begin_row, BLK, 0), "ctx", owner),
            broadcast(lax.dynamic_slice_in_dim(value_feat, begin_row, BLK, 0), "ctx", owner),
        )
        global_key_list.append(got_key)
        global_value_list.append(got_value)
    global_keys = jnp.stack(global_key_list).reshape(NGLOB, BLK, heads_here, HS)
    global_values = jnp.stack(global_value_list).reshape(NGLOB, BLK, heads_here, HS)
    own_lists = lax.dynamic_slice_in_dim(block_lists, first_block, blocks_here, 0)
    global_ok = own_lists[:, BAND:] >= 0
    global_scores = jnp.einsum(
        "bqhd,skhd->bhqsk", query_blocks, global_keys, preferred_element_type=jnp.float32
    ) / math.sqrt(HS)
    global_scores = jnp.where(global_ok[:, None, None, :, None], global_scores, -jnp.inf)
    row_top = jnp.maximum(row_top, jnp.max(global_scores, axis=(3, 4)))
    global_weights = jnp.exp(global_scores - row_top[:, :, :, None, None])
    denominator = jnp.sum(global_weights, axis=(3, 4))
    numerator = jnp.einsum(
        "bhqsk,skhd->bqhd",
        global_weights.astype(jnp.bfloat16),
        global_values,
        preferred_element_type=jnp.float32,
    )
    for band_step in range(BAND):
        weights = jnp.exp(band_scores[band_step] - row_top[:, :, :, None])
        denominator = denominator + jnp.sum(weights, axis=3)
        numerator = numerator + jnp.einsum(
            "bhqk,bkhd->bqhd",
            weights.astype(jnp.bfloat16),
            band_values[band_step],
            preferred_element_type=jnp.float32,
        )
    attended = (numerator / jnp.transpose(denominator, (0, 2, 1))[:, :, :, None]).reshape(
        row_count, width_here
    )
    energy_sum = lax.psum(jnp.sum(attended * attended, axis=1), "head")
    return (attended * out_gain * lax.rsqrt(energy_sum / D + 1e-06)[:, None]).astype(jnp.bfloat16)


def solution(mesh):
    placed = (
        P("ctx", "head"),
        P("ctx", "head"),
        P("ctx", "head"),
        P("ctx", "head"),
        P(None, None, "head"),
        P(None, "head"),
        P("head"),
        P(),
    )
    return jax.shard_map(
        per_device, mesh=mesh, in_specs=placed, out_specs=P("ctx", "head"), check_vma=False
    )
```

profile of v0, /device:TPU:4, one launch (start us, length us, event | category | flops | bytes accessed | tf_op | source)
XLA Modules:
  0.0 1202.6 jit_solution(13187844340905520926)
XLA Ops:
  6.5 0.9 slice.184
  7.5 1.1 copy.147
  8.5 2.5 collective-permute-start.3
  11.1 0.8 slice.164
  11.9 1.1 copy.142
  12.9 4.1 collective-permute-start.1
  17.0 0.8 slice.158
  17.8 1.1 copy.139
  18.8 2.1 collective-permute-start
  20.9 1.2 fusion.87
  22.1 1.2 fusion.88
  29.1 1.5 copy.138
  30.8 5.0 add_multiply_fusion
  35.8 1.3 copy-done
  37.8 3.0 collective-permute-start.2
  40.7 3.3 add_convert_fusion.1
  44.4 1.0 copy.152
  45.5 1.0 copy.151
  46.5 1.0 copy.150
  47.5 1.0 copy.149
  48.9 12.6 %fusion.13 = bf16[256,2048]{0,1:T(8,128)(2,1)S(1)} fusion(f32[256,2048]{0,1:T(8,128)} %copy-done, f32[6,2048]{0,1:T(8,128)S(1)} %copy.145, f32[2048]{0:T(1024)S(1)} %bitcast.119, f32[2048]{0:T(1024)S(1)} %bitcast.120, f32[2048]{0:T(1024)S(1)} %bitcast.115, f32[2048]{0:T(1024)S(1)} %bitcast.116, f32[2048]{0:T(1024)S(1)} %bitcast.117, f32[2048]{0:T(1024)S(1)} %bitcast.118, ...), kind=kLoop, calls=%fused_computation.24 | loop fusion | flops 10485760 | bytes 3252224 | tf_op jit(solution)/shard_map/convert_element_type | solution.py:66
  61.5 1.6 dynamic-slice_select_fusion.7
  63.1 0.8 slice.190
  63.9 2.7 collective-permute-start.4
  66.8 3.2 collective-permute-start.5
  70.1 1.1 reshape.128
  71.2 3.2 fusion.75
  74.6 2.2 fusion.49
  76.9 3.7 collective-permute-start.6
  80.5 1.2 bitcast_bitcast_fusion
  81.7 1.1 reshape.131
  82.8 1.1 pad_maximum_fusion.2
  83.9 2.2 reshape.138
  86.1 1.1 reshape.137
  87.2 3.6 fusion.47
  90.8 2.3 fusion.48
  93.1 1.2 pad_maximum_fusion.1
  94.6 1.4 reshape.139
  96.0 1075.3 %all-reduce.3.cloned.1.call-done = (bf16[1,128,16,128]{3,1,0,2:T(8,128)(2,1)}, bf16[1,128,16,128]{3,1,0,2:T(8,128)(2,1)}, bf16[1,128,16,128]{3,1,0,2:T(8,128)(2,...) async-done(((bf16[1,128,16,128]{3,1,0,2:T(8,128)(2,1)}, ...) | async-done | bytes 4194320 | tf_op jit(solution)/shard_map/psum | solution.py:25
  1171.3 2.8 fusion.2
  1174.2 1.8 fusion
  1176.4 0.6 copy-done.5
  1177.0 1.9 fusion.50
  1181.0 2.0 fusion.3
  1183.0 2.2 multiply_reduce_fusion
  1185.2 2.3 copy.175
  1187.5 6.5 psum.71
  1193.9 1.8 fusion.27
  (65 shorter events, 6.3 us)
Async XLA Ops:
  6.5 16.8 %copy-start.6 = (bf16[256,2048]{1,0:T(8,128)(2,1)S(1)}, bf16[256,2048]{1,0:T(8,128)(2,1)}, u32[]{:S(2)}) copy-start(bf16[256,2048]{1,0:T(8,128)(2,1)} %param.9) | copy-start | bytes 3145732
  6.5 22.1 %copy-start.7 = (bf16[256,2048]{1,0:T(8,128)(2,1)S(1)}, bf16[256,2048]{1,0:T(8,128)(2,1)}, u32[]{:S(2)}) copy-start(bf16[256,2048]{1,0:T(8,128)(2,1)} %param.10) | copy-start | bytes 3145732
  6.5 17.4 %copy-start.13 = (s32[256,7]{0,1:T(8,128)S(1)}, s32[256,7]{0,1:T(8,128)}, u32[]{:S(2)}) copy-start(s32[256,7]{0,1:T(8,128)} %param.15) | copy-start | bytes 21508
  6.5 1164.8 %all-reduce.3.cloned.1.call-start = ((), (), s32[]{:S(2)}) async-start(), calls=%async_computation | async-start | bytes 8388608 | tf_op jit(solution)/shard_map/psum | solution.py:25
  8.5 32.2 %collective-permute-start.3 = (bf16[2,2048]{0,1:T(8,128)(2,1)}, bf16[2,2048]{0,1:T(8,128)(2,1)}, u32[]{:S(2)}, u32[]{:S(2)}) collective-permute-start(bf16[2,2048]{0,1:T(8,128)(2,1)} %copy.147), channel_id=1, source_target_pairs={{0,2},{2,4},{4,6},{6,8},{8,10},{10,12},{12,14},{14,16},{16,18},{18... | collective-permute-start | bytes 24584 | tf_op jit(solution)/shard_map/ppermute | solution.py:20
  12.9 17.8 %collective-permute-start.1 = (bf16[2,2048]{0,1:T(8,128)(2,1)}, bf16[2,2048]{0,1:T(8,128)(2,1)}, u32[]{:S(2)}, u32[]{:S(2)}) collective-permute-start(bf16[2,2048]{0,1:T(8,128)(2,1)} %copy.142), channel_id=1, source_target_pairs={{0,2},{2,4},{4,6},{6,8},{8,10},{10,12},{12,14},{14,16},{16,18},{18... | collective-permute-start | bytes 24584 | tf_op jit(solution)/shard_map/ppermute | solution.py:20
  18.8 11.9 collective-permute-start
  35.7 1.3 copy-start
  37.8 10.7 collective-permute-start.2
  63.9 7.3 collective-permute-start.4
  66.8 16.0 %collective-permute-start.5 = (bf16[256,2048]{0,1:T(8,128)(2,1)S(1)}, bf16[256,2048]{0,1:T(8,128)(2,1)S(1)}, u32[]{:S(2)}, u32[]{:S(2)}) collective-permute-start(bf16[256,2048]{0,1:T(8,128)(2,1)S(1)} %add_convert_fusion.1), channel_id=1, source_target_pairs={{0,2},{2,4},{4,6},{6,8},{8,10},{10,12},{12,14},{14,16},{16,18},{18... | collective-permute-start | bytes 3145736 | tf_op jit(solution)/shard_map/ppermute | solution.py:20
  71.2 3.4 copy-start.10
  74.6 5.9 copy-start.1
  76.9 16.2 %collective-permute-start.6 = (bf16[256,2048]{0,1:T(8,128)(2,1)S(1)}, bf16[256,2048]{0,1:T(8,128)(2,1)}, u32[]{:S(2)}, u32[]{:S(2)}) collective-permute-start(bf16[256,2048]{0,1:T(8,128)(2,1)S(1)} %fusion.13), channel_id=1, source_target_pairs={{0,2},{2,4},{4,6},{6,8},{8,10},{10,12},{12,14},{14,16},{16,18},{18... | collective-permute-start | bytes 3145736 | tf_op jit(solution)/shard_map/ppermute | solution.py:20
  83.9 3.3 copy-start.2
  87.2 3.6 copy-start.11
  94.5 1076.8 %copy-start.9 = (bf16[2,128,16,128,1]{3,2,1,0,4:T(8,128)(2,1)S(1)}, bf16[2,128,16,128,1]{3,2,1,0,4:T(8,128)(2,1)}, u32[]{:S(2)}) copy-start(bf16[2,128,16,128,1]{3,2,1,0,4:T(8,128)(2,1)} %bitcast_bitcast_fusion) | copy-start | bytes 3145732
  1174.2 1.8 copy-start.3
  1174.2 2.2 copy-start.4
  1174.2 2.8 copy-start.5
  1179.4 1.0 copy-start.14
  1179.4 1.2 copy-start.15
  1179.5 1.3 copy-start.16
  1179.5 1.5 copy-start.17
  1181.0 2.0 copy-start.8
  1185.2 8.7 copy-start.12
Sparse Core Ops, SparseCore 0:
  63.3 1108.0 all-reduce.2
where the time goes:
time: 1200 us
  waiting for transfers between devices  1080 us (90%)
  other arithmetic  34 us (3%)
  local copies, waits for them, and re-layouts  31.5 us (3%)
  starting transfers between devices  21.3 us (2%)
  between operations  18 us (2%)
  matrix products  16 us (1%)
    psum x1, waiting for transfers between devices, broadcast(): return lax.psum(kept, axis)  1080 us
  transfers between devices with their start and end apart: 8, of which 1 were waited for; matrix products, arithmetic and copies ran while one was open for 4% of the time, Pallas kernels for 0%

commit v1 on v0

v1 whole, which is shorter than its diff:
```python
import functools
import math

import jax
import jax.numpy as jnp
from jax import lax
from jax.experimental import pallas as pl
from jax.experimental.pallas import tpu as pltpu
from jax.sharding import PartitionSpec as P

D = 4096
HS = 128
BLK = 128
BAND = 3
NGLOB = 4
TAPS = 3
TAPS_LONG = 7
ROWS = 256
HEADS_HERE = 16
HALF = 8
HALO = 16
PART = 64
MESH = pl.DeviceIdType.MESH
F32 = jnp.float32
BF16 = jnp.bfloat16
VMEM = pltpu.VMEM
MIB = 1024 * 1024


def taps_of(ext, weights, count):
    total = weights[0:1] * ext
    for s in range(1, count):
        total = total + weights[s : s + 1] * pltpu.roll(ext, s, 0)
    return total


def features_kernel(
    parity_ref, q_ref, k_ref, v_ref, g_ref, sf_ref, lf_ref,
    qf_ref, kv_ref, cand_ref, halo, send_sem, recv_sem,
):
    me = lax.axis_index("ctx")
    last = lax.axis_size("ctx") - 1
    streams = (q_ref, k_ref, v_ref, g_ref)
    barrier = pltpu.get_barrier_semaphore()

    for other in ((me + last) % (last + 1), (me + 1) % (last + 1)):
        pl.semaphore_signal(barrier, inc=1, device_id={"ctx": other}, device_id_type=MESH)
    pl.semaphore_wait(barrier, 2)

    def tail_copy(i):
        return pltpu.make_async_remote_copy(
            src_ref=streams[i].at[pl.ds(ROWS - HALO, HALO)],
            dst_ref=halo.at[i],
            send_sem=send_sem.at[i],
            recv_sem=recv_sem.at[i],
            device_id={"ctx": me + 1},
            device_id_type=MESH,
        )

    @pl.when(me < last)
    def _():
        for i in range(4):
            tail_copy(i).start()

    @pl.when(me == 0)
    def _():
        halo[...] = jnp.zeros_like(halo)

    def part(h, r):
        cols = pl.ds(pl.multiple_of(h * HS, HS), HS)

        def extended(i):
            if r == 0:
                before = halo[i, :, cols].astype(F32)
                return jnp.concatenate([before, streams[i][0:PART, cols].astype(F32)], 0)
            return streams[i][r * PART - HALO : (r + 1) * PART, cols].astype(F32)

        feats = [taps_of(extended(i), sf_ref[i, :, cols], TAPS) for i in range(4)]
        values = taps_of(feats[3] * feats[2], lf_ref[:, cols], TAPS_LONG)
        qf_ref[h, r * PART : (r + 1) * PART, :] = feats[0][HALO:].astype(BF16)
        low = r * PART % BLK
        kv_ref[r * PART // BLK, h, 0, low : low + PART, :] = feats[1][HALO:].astype(BF16)
        kv_ref[r * PART // BLK, h, 1, low : low + PART, :] = values[HALO:].astype(BF16)

    @pl.loop(0, HEADS_HERE)
    def _(h):
        for r in range(1, ROWS // PART):
            part(h, r)

    @pl.when(me > 0)
    def _():
        for i in range(4):
            tail_copy(i).wait_recv()

    parity = parity_ref[0]

    @pl.loop(0, HEADS_HERE)
    def _(h):
        part(h, 0)
        cand_ref[h] = kv_ref[parity, h]

    @pl.when(me < last)
    def _():
        for i in range(4):
            tail_copy(i).wait_send()


def features(parity, q_raw, k_raw, v_raw, g_raw, short_filters, long_filter):
    vm = pl.BlockSpec(memory_space=VMEM)
    return pl.pallas_call(
        features_kernel,
        out_shape=(
            jax.ShapeDtypeStruct((HEADS_HERE, ROWS, HS), BF16),
            jax.ShapeDtypeStruct((2, HEADS_HERE, 2, BLK, HS), BF16),
            jax.ShapeDtypeStruct((HEADS_HERE, 2, BLK, HS), BF16),
        ),
        in_specs=[pl.BlockSpec(memory_space=pltpu.SMEM)] + [vm] * 6,
        out_specs=(vm, vm, vm),
        scratch_shapes=[
            VMEM((4, HALO, HEADS_HERE * HS), BF16),
            pltpu.SemaphoreType.DMA((4,)),
            pltpu.SemaphoreType.DMA((4,)),
        ],
        compiler_params=pltpu.CompilerParams(
            collective_id=0, has_side_effects=True, vmem_limit_bytes=32 * MIB
        ),
        name="features",
    )(parity, q_raw, k_raw, v_raw, g_raw, short_filters, long_filter)


def exchange_kernel(source, kv_ref, cand_ref, band_ref, glob_ref, send_sem, recv_sem, band_send, band_recv, fill_sem):
    x0, z0, c0 = source // 16, source // 2 % 8, source % 2
    me = lax.axis_index("ctx")
    last = lax.axis_size("ctx") - 1
    core = me % 2
    z = me // 2 % 8
    x = me // 16 % 2
    y = me // 32
    steps = (z0 - z + 8) % 8

    def at(yy, xx, zz, cc):
        return ((yy * 2 + xx) * 8 + zz) * 2 + cc

    z_up, z_down = at(y, x, (z + 1) % 8, core), at(y, x, (z + 7) % 8, core)
    x_other = at(y, 1 - x, z, core)
    y_up, y_down = at((y + 1) % 4, x, z, core), at((y + 3) % 4, x, z, core)
    sibling = at(y, x, z, 1 - core)
    outer = (me + last + 2 * core) % (last + 1)

    barrier = pltpu.get_barrier_semaphore()
    for other in (z_up, z_down, x_other, y_up, y_down, sibling, outer):
        pl.semaphore_signal(barrier, inc=1, device_id={"ctx": other}, device_id_type=MESH)
    pl.semaphore_wait(barrier, 7)

    def band_copy():
        return pltpu.make_async_remote_copy(
            src_ref=kv_ref, dst_ref=band_ref, send_sem=band_send, recv_sem=band_recv,
            device_id={"ctx": me + 1}, device_id_type=MESH,
        )

    @pl.when(me < last)
    def _():
        band_copy().start()

    @pl.when(me == 0)
    def _():
        pltpu.make_async_copy(kv_ref, band_ref, band_recv).start()

    main = x == (x0 + core) % 2
    at_source = (x == x0) & (steps == 0)
    mine, theirs = core * HALF, (1 - core) * HALF

    plans = []
    for s in range(NGLOB):
        plane = y == s
        down_z = plane & main & (steps < 7)
        over_x = plane & (
            (main & jnp.logical_not((core == 1) & (steps == 0)))
            | (jnp.logical_not(main) & (core == 1) & (steps == 0))
        )
        never = y < 0
        up = [
            (y == 0) | ((y == 1) & (core == 0)),
            (y == 1) | ((y == 2) & (core == 0)),
            y == 2,
            never,
        ][s]
        down = [
            (y == 0) | ((y == 3) & (core == 1)),
            ((y == 1) | (y == 0)) & (core == 1),
            never,
            never,
        ][s]
        needs = y >= s
        owner = plane & at_source & (core == c0)
        near_owner = plane & at_source & (core != c0)
        holds = needs if s != 1 else (needs | ((y == 0) & (core == 1)))
        share = needs & jnp.logical_not(near_owner)
        routes = []
        if s < 3:
            routes += [(2, up, y_up)]
        if s < 2:
            routes += [(3, down, y_down)]
        routes = [(0, down_z, z_down), (1, over_x, x_other)] + routes + [(4, share, sibling)]
        plans.append((needs, owner, holds, routes))

    def send(s, h, kind, target):
        return pltpu.make_async_remote_copy(
            src_ref=glob_ref.at[s, h], dst_ref=glob_ref.at[s, h],
            send_sem=send_sem.at[s, kind], recv_sem=recv_sem.at[s, h],
            device_id={"ctx": target}, device_id_type=MESH,
        )

    def sent(s, kind, first):
        span = glob_ref.at[s, pl.ds(first, HALF)]
        return pltpu.make_async_remote_copy(
            src_ref=span, dst_ref=span,
            send_sem=send_sem.at[s, kind], recv_sem=recv_sem.at[s, 0],
            device_id={"ctx": sibling}, device_id_type=MESH,
        )

    for s in range(NGLOB):
        needs, owner, holds, routes = plans[s]

        @pl.when(owner)
        def _():
            @pl.loop(0, HEADS_HERE)
            def _(h):
                pltpu.make_async_copy(cand_ref.at[h], glob_ref.at[s, h], recv_sem.at[s, h]).start()

        @pl.when(jnp.logical_not(needs))
        def _():
            span = pl.ds(theirs, HALF)
            pltpu.make_async_copy(cand_ref.at[span], glob_ref.at[s, span], fill_sem.at[s, 0]).start()

        @pl.when(jnp.logical_not(holds))
        def _():
            span = pl.ds(mine, HALF)
            pltpu.make_async_copy(cand_ref.at[span], glob_ref.at[s, span], fill_sem.at[s, 1]).start()

    @pl.loop(0, HALF)
    def _(j):
        for s in range(NGLOB):
            needs, owner, holds, routes = plans[s]

            @pl.when(holds)
            def _():
                h = mine + j
                send(s, h, 0, sibling).wait_recv()
                for kind, on, target in routes:

                    @pl.when(on)
                    def _():
                        send(s, h, kind, target).start()

            @pl.when(owner)
            def _():
                h = theirs + j
                send(s, h, 5, sibling).wait_recv()
                send(s, h, 5, sibling).start()

    for s in range(NGLOB):
        needs, owner, holds, routes = plans[s]

        @pl.when(needs & jnp.logical_not(owner))
        def _():
            @pl.loop(0, HALF)
            def _(j):
                send(s, theirs + j, 0, sibling).wait_recv()

        @pl.when(owner)
        def _():
            sent(s, 5, theirs).wait_send()

        for kind, on, target in routes:

            @pl.when(on)
            def _():
                sent(s, kind, mine).wait_send()

        @pl.when(jnp.logical_not(needs))
        def _():
            span = pl.ds(theirs, HALF)
            pltpu.make_async_copy(cand_ref.at[span], glob_ref.at[s, span], fill_sem.at[s, 0]).wait()

        @pl.when(jnp.logical_not(holds))
        def _():
            span = pl.ds(mine, HALF)
            pltpu.make_async_copy(cand_ref.at[span], glob_ref.at[s, span], fill_sem.at[s, 1]).wait()

    @pl.when(me < last)
    def _():
        band_copy().wait_send()

    band_copy().wait_recv()


def exchange(source, kv, cand):
    hbm = pl.BlockSpec(memory_space=pl.ANY)
    return pl.pallas_call(
        functools.partial(exchange_kernel, source),
        out_shape=(
            jax.ShapeDtypeStruct((2, HEADS_HERE, 2, BLK, HS), BF16),
            jax.ShapeDtypeStruct((NGLOB, HEADS_HERE, 2, BLK, HS), BF16),
        ),
        in_specs=[hbm, hbm],
        out_specs=(hbm, hbm),
        scratch_shapes=[
            pltpu.SemaphoreType.DMA((NGLOB, 6)),
            pltpu.SemaphoreType.DMA((NGLOB, HEADS_HERE)),
            pltpu.SemaphoreType.DMA,
            pltpu.SemaphoreType.DMA,
            pltpu.SemaphoreType.DMA((NGLOB, 2)),
        ],
        compiler_params=pltpu.CompilerParams(collective_id=2 + source, has_side_effects=True),
        name=f"exchange_{source}",
    )(kv, cand)


def attention_kernel(
    bias_ref, q_ref, kv_ref, band_ref, glob_ref, gain_ref, out_ref,
    att, square, mine, theirs, send_sem, recv_sem,
):
    h = pl.program_id(0)
    me = lax.axis_index("ctx")
    partner = 1 - lax.axis_index("head")
    barrier = pltpu.get_barrier_semaphore()

    @pl.when(h == 0)
    def _():
        pl.semaphore_signal(barrier, inc=1, device_id={"head": partner}, device_id_type=MESH)
        square[...] = jnp.zeros_like(square)

    edge = jnp.where(me == 0, -jnp.inf, 0.0).astype(F32)
    rows = lax.broadcasted_iota(jnp.int32, (BLK, BLK), 0)
    cols = lax.broadcasted_iota(jnp.int32, (BLK, BLK), 1)
    causal = rows >= cols
    scale = math.log2(math.e) / math.sqrt(HS)
    pieces = []
    for b in range(2):
        q = q_ref[0, b * BLK : (b + 1) * BLK, :]
        if b == 0:
            blocks = [(band_ref.at[0], edge), (band_ref.at[1], edge), (kv_ref.at[0], causal)]
        else:
            blocks = [(band_ref.at[1], edge), (kv_ref.at[0], None), (kv_ref.at[1], causal)]
        blocks += [(glob_ref.at[s], bias_ref[b, s]) for s in range(NGLOB)]
        scores = []
        for ref, mask in blocks:
            one = lax.dot_general(q, ref[0, 0], (((1,), (1,)), ((), ())), preferred_element_type=F32)
            if mask is causal:
                one = jnp.where(causal, one, -jnp.inf)
            elif mask is not None:
                one = one + mask
            scores.append(one)
        top = scores[0]
        for one in scores[1:]:
            top = jnp.maximum(top, one)
        top = jnp.max(top, axis=1, keepdims=True)
        total = None
        blend = None
        for (ref, mask), one in zip(blocks, scores):
            weight = jnp.exp2((one - top) * scale)
            total = weight if total is None else total + weight
            term = jnp.dot(weight.astype(BF16), ref[0, 1], preferred_element_type=F32)
            blend = term if blend is None else blend + term
        total = jnp.sum(total, axis=1, keepdims=True)
        value = blend / total
        att[h, b * BLK : (b + 1) * BLK, :] = value
        pieces.append(value * value)
    square[...] += jnp.concatenate(pieces, 0)

    @pl.when(h == HEADS_HERE - 1)
    def _():
        mine[...] = lax.dot_general(
            jnp.ones((8, HS), F32), square[...], (((1,), (1,)), ((), ())),
            preferred_element_type=F32, precision=lax.Precision.HIGHEST,
        )
        pl.semaphore_wait(barrier, 1)
        copy = pltpu.make_async_remote_copy(
            src_ref=mine, dst_ref=theirs, send_sem=send_sem, recv_sem=recv_sem,
            device_id={"head": partner}, device_id_type=MESH,
        )
        copy.start()
        copy.wait()
        factor = lax.rsqrt((mine[...] + theirs[...]) / D + 1e-06)
        column = jnp.transpose(factor)[:, 0:1]
        for i in range(HEADS_HERE):
            span = slice(i * HS, (i + 1) * HS)
            out_ref[:, span] = (att[i] * gain_ref[:, span] * column).astype(BF16)


def attention(bias, qf, kv, band, glob, gain):
    def per_head(shape, place):
        def index(h):
            return tuple(h if i == place else 0 for i in range(len(shape)))

        return pl.BlockSpec(shape, index)

    whole = HEADS_HERE * HS
    return pl.pallas_call(
        attention_kernel,
        grid=(HEADS_HERE,),
        out_shape=jax.ShapeDtypeStruct((ROWS, whole), BF16),
        in_specs=[
            pl.BlockSpec(memory_space=pltpu.SMEM),
            per_head((1, ROWS, HS), 0),
            per_head((2, 1, 2, BLK, HS), 1),
            per_head((2, 1, 2, BLK, HS), 1),
            per_head((NGLOB, 1, 2, BLK, HS), 1),
            pl.BlockSpec((1, whole), lambda h: (0, 0)),
        ],
        out_specs=pl.BlockSpec((ROWS, whole), lambda h: (0, 0)),
        scratch_shapes=[
            VMEM((HEADS_HERE, ROWS, HS), F32),
            VMEM((ROWS, HS), F32),
            VMEM((8, ROWS), F32),
            VMEM((8, ROWS), F32),
            pltpu.SemaphoreType.DMA,
            pltpu.SemaphoreType.DMA,
        ],
        compiler_params=pltpu.CompilerParams(
            collective_id=1, has_side_effects=True, vmem_limit_bytes=32 * MIB
        ),
        name="attention",
    )(bias, qf, kv, band, glob, gain)


def per_device(q_raw, k_raw, v_raw, g_raw, short_filters, long_filter, out_gain, block_lists):
    phase = block_lists[block_lists.shape[0] - 1, BAND]
    first = lax.axis_index("ctx") * 2
    own = lax.dynamic_slice_in_dim(block_lists, first, 2, 0)[:, BAND:]
    bias = jnp.where(own >= 0, 0.0, -jnp.inf).astype(F32)
    parity = jnp.reshape(phase % 2, (1,))
    qf, kv, cand = features(parity, q_raw, k_raw, v_raw, g_raw, short_filters, long_filter)
    band, glob = lax.switch(
        phase // 2, [functools.partial(exchange, source) for source in range(31)], kv, cand
    )
    return attention(bias, qf, kv, band, glob, out_gain[None, :])


def solution(mesh):
    placed = (
        P("ctx", "head"),
        P("ctx", "head"),
        P("ctx", "head"),
        P("ctx", "head"),
        P(None, None, "head"),
        P(None, "head"),
        P("head"),
        P(),
    )
    return jax.shard_map(
        per_device, mesh=mesh, in_specs=placed, out_specs=P("ctx", "head"), check_vma=False
    )
```

time: 1200 us -> 179 us (0.15)
  the two profiles are of different devices: /device:TPU:4 before, /device:TPU:96 now
where the time goes in v1:
time: 179 us; the launch traced here: 178 us
  Pallas kernels  166 us (93%)
  local copies, waits for them, and re-layouts  9.13 us (5%)
  between operations  2.7 us (2%)
    pallas_call x1, Pallas kernels, exchange(): pl.pallas_call(functools.partial(exchange_kernel, source), out_shape=(jax...  134 us
    pallas_call x1, Pallas kernels, attention(): pl.pallas_call(attention_kernel, grid=(HEADS_HERE,), out_shape=jax.ShapeD...  24.5 us
    pallas_call x1, Pallas kernels, features(): pl.pallas_call(features_kernel, out_shape=(jax.ShapeDtypeStruct((HEADS_HE...  8.27 us
    unnamed x17, local copies, waits for them, and re-layouts  7.78 us

profile of v1, /device:TPU:96, one launch (start us, length us, event | category | flops | bytes accessed | tf_op | source)
XLA Modules:
  0.0 178.4 jit_solution(13426211322168629690)
XLA Ops:
  0.0 1.3 slice.7
  3.2 1.0 copy.10.sf_ref
  4.2 0.0 copy-start
  4.2 1.2 copy-done
  5.4 0.0 copy-start.1
  5.4 1.2 copy-done.1
  6.6 0.0 copy-start.2
  6.6 1.2 copy-done.2
  7.9 0.0 copy-start.3
  7.9 1.2 copy-done.3
  9.1 0.0 copy-start.4
  9.1 0.8 copy-done.4
  9.9 8.3 %features.1 = (bf16[16,256,128]{2,1,0:T(8,128)(2,1)S(1)}, bf16[2,16,2,128,128]{4,3,2,1,0:T(8,128)(2,1)S(1)}, bf16[16,2,128,128]{3,2,1,0:T(8,128)(2,1)}) custom-call(s32[1]{0:T(128)} %bitcast.1.parity_ref, bf16[256,2048]{1,0:T(8,128)(2,1)S(1)} %copy-done, bf16[256,2048]{1,0:T(8,128)(2,1)S(1)} %copy-done.1, bf16[256,2048]{1,0:T(8,128)(2,1)S(1)} %copy-done.2, ...), custom_call_target="tpu_custom_call" | custom-call | tf_op jit(solution)/shard_map/features/pallas_call | solution.py:110
  18.9 0.0 copy-start.6
  18.9 0.0 copy-start.5
  18.9 133.8 %conditional.1 = ((bf16[2,16,2,128,128]{4,3,2,1,0:T(8,128)(2,1)}, bf16[4,16,2,128,128]{4,3,2,1,0:T(8,128)(2,1)})) conditional(s32[]{:T(128)} %clamp.3, (bf16[2,16,2,128,128]{4,3,2,1,0:T(8,128)(2,1)S(1)}, bf16[16,2,128,128]{3,2,1,0:T(8,128)(2,1)}) %tuple.98, (bf16[2,16,2,128,128]{4,3,2,1,0:T(8,128)(2,1)S(1)}, ...), branch_computations={%region_0.1_spmd, %region_1.2_spmd, %region_2.3_spmd, %region_3.4_... | conditional | bytes 8 | solution.py:435
  19.0 133.6 %exchange_6.1 = (bf16[2,16,2,128,128]{4,3,2,1,0:T(8,128)(2,1)}, bf16[4,16,2,128,128]{4,3,2,1,0:T(8,128)(2,1)}) custom-call(bf16[2,16,2,128,128]{4,3,2,1,0:T(8,128)(2,1)S(1)} %get-tuple-element.141.kv_ref, bf16[16,2,128,128]{3,2,1,0:T(8,128)(2,1)} %get-tuple-element.142.cand_ref), custom_call_target="tpu_custom_call" | custom-call | tf_op jit(solution)/shard_map/cond/branch_6_fun/exchange_6/pallas_call | solution.py:300
  152.7 0.0 copy-done.6
  152.8 0.1 constant_dynamic-slice_fusion
  152.8 0.1 copy.12
  152.9 0.0 copy-done.5
  152.9 24.5 %attention.1 = bf16[256,2048]{1,0:T(8,128)(2,1)S(1)} custom-call(f32[2,4]{1,0:T(2,128)S(1)} %compare_select_fusion.bias_ref, bf16[16,256,128]{2,1,0:T(8,128)(2,1)S(1)} %get-tuple-element.196.q_ref, bf16[2,16,2,128,128]{4,3,2,1,0:T(8,128)(2,1)S(1)} %get-tuple-element.197.kv_ref, bf16[2,16,2,128,128]{4,3,2,1,0:T(8,128)(2,1)} %get-tuple-element.199.band_ref, ...), custom_call_target="tpu_custom_call" | custom-call | tf_op jit(solution)/shard_map/attention/pallas_call | solution.py:400
  177.5 1.0 copy.76
  (2 shorter events, 0.0 us)
Async XLA Ops:
  4.2 1.2 copy-start
  5.4 1.2 copy-start.1
  6.6 1.2 copy-start.2
  7.9 1.2 copy-start.3
  9.1 0.8 copy-start.4
  18.9 133.9 %copy-start.6 = (s32[256,7]{0,1:T(8,128)S(1)}, s32[256,7]{0,1:T(8,128)}, u32[]{:S(2)}) copy-start(s32[256,7]{0,1:T(8,128)} %param.46) | copy-start | bytes 21508
  18.9 134.0 %copy-start.5 = (f32[2048]{0:T(1024)S(1)}, f32[2048]{0:T(1024)}, u32[]{:S(2)}) copy-start(f32[2048]{0:T(1024)} %param.45) | copy-start | bytes 24580
